TPU v7x, 32 devices: a whole 2x2x4 slice. The times are simulated.
32 devices in a mesh: term: 8 (over z, y), sector: 4 (over x, core).
Axes of the slice: x: 2, y: 2, z: 4, core: 2. Of those that a mesh axis runs over, the one named last changes fastest.
Arguments:
- wavefunction: bfloat16 [512, 128, 128], P(('term', 'sector')), may hold values from -6 to 6
- left_sector: int32 [512, 1], P(('term', 'sector')), may hold values from 0 to 3; in each aligned block of 16 rows (0 to 15, 16 to 31, ...) at most 8 rows name the same one
- right_sector: int32 [512], P(('term', 'sector')), may hold values from 0 to 3
- left_blocks: bfloat16 [16, 4, 128, 128], P('term', 'sector'), may hold values from -0.5 to 0.5
- right_blocks: bfloat16 [16, 4, 128, 128], P('term'), may hold values from -0.125 to 0.125
Outputs:
- product_blocks: bfloat16 [512, 128, 128], P(('term', 'sector'))
Inputs may be any that keep to these rules, and one draw needn't show every extreme that they name: `left_sector`: among the 16 blocks of one device no left sector is named more than 8 times, and some left sector is named exactly 8 times.
All inputs are finite; a program needn't handle non-finite values.
Results may differ from a plain program's by a relative error of at most 0.0049.
Values may be sent and summed in bfloat16 or wider, within the bound.
No kernel may reach another device: no remote copies, remote signals or barrier semaphores. Data moves between devices by JAX's collectives and lax.ppermute only.
A program may use at most 64 MiB of HBM per device.

v0:
```python
import math

import jax
import jax.numpy as jnp
from jax import lax
from jax.experimental import pallas as pl
from jax.experimental.pallas import tpu as pltpu
from jax.sharding import PartitionSpec as P


def neighbour_ring(n):
    return list(range(0, n, 2)) + list(range(1, n, 2))[::-1]


def along_ring(block, ring):
    n, n_sec = len(ring), lax.axis_size("sector")
    route = []
    for at in range(n):
        for sector in range(n_sec):
            to = (at + (1 if sector % 2 == 0 else -1)) % n
            route.append((ring[at] * n_sec + sector, ring[to] * n_sec + sector))
    return lax.ppermute(block, ("term", "sector"), route)


def from_sector(block, offset):
    n = lax.axis_size("sector")
    return lax.ppermute(block, "sector", [(i, i ^ offset) for i in range(n)])


def apply_groups(parts, table, groups, n_left, n_right, out_dtype=jnp.float32):
    held, order = parts[0][1].shape[:2]
    n_parts, n_groups = len(parts), len(groups)
    fresh = parts[0][0] is None
    together = math.gcd(held, 16)
    terms = [(g, t) for g, group in enumerate(groups) for t in range(group[2])]

    def kernel(*refs):
        table_ref, refs = refs[0], refs[1:]
        group_refs = refs[: n_groups * 2]
        wave_refs = refs[n_groups * 2 : n_groups * 2 + n_parts]
        total_refs = refs[n_groups * 2 + n_parts : -n_parts]
        out_refs = refs[-n_parts:]

        def operator(side, n_slots, g, t, slot):
            ref = group_refs[2 * g + side]
            skip = table_ref[4, 0] if ref.shape[0] > groups[g][2] * n_slots else 0
            return ref[(skip + t) * n_slots + slot]

        def work_on(p, first):
            blocks = [first + i for i in range(together)]
            mixed = []
            for k in blocks:
                slot = table_ref[parts[p][2], k]
                lefts = [operator(0, n_left, g, t, slot) for g, t in terms]
                mixed.append(
                    jnp.dot(
                        jnp.concatenate(lefts, axis=0), wave_refs[p][k], preferred_element_type=jnp.float32
                    ).astype(jnp.bfloat16)
                )
            added = []
            for k, one in zip(blocks, mixed):
                slot = table_ref[parts[p][2] + 1, k]
                rights = [operator(1, n_right, g, t, slot) for g, t in terms]
                wide = jnp.concatenate(
                    [one[i * order : (i + 1) * order] for i in range(len(terms))], axis=1
                )
                added.append(
                    jnp.dot(wide, jnp.concatenate(rights, axis=0), preferred_element_type=jnp.float32)
                )
            for k, one in zip(blocks, added):
                total = one if fresh else total_refs[p][k] + one
                out_refs[p][k] = total.astype(out_dtype)

        for p in range(n_parts):
            for first in range(0, held, together):
                work_on(p, first)

    smem = pl.BlockSpec(memory_space=pltpu.SMEM)
    vmem = pl.BlockSpec(memory_space=pltpu.VMEM)
    operands = [table] + [x for group in groups for x in group[:2]] + [part[1] for part in parts]
    aliases = {}
    if not fresh:
        if out_dtype == jnp.float32:
            aliases = {len(operands) + p: p for p in range(n_parts)}
        operands += [part[0] for part in parts]
    nbytes = sum(x.size * x.dtype.itemsize for x in operands)
    waves = sum(part[1].size for part in parts)
    return pl.pallas_call(
        kernel,
        out_shape=[jax.ShapeDtypeStruct(part[1].shape, out_dtype) for part in parts],
        in_specs=[smem] + [vmem] * (len(operands) - 1),
        out_specs=[vmem] * n_parts,
        input_output_aliases=aliases,
        compiler_params=pltpu.CompilerParams(vmem_limit_bytes=nbytes + 4 * waves + (8 << 20)),
        cost_estimate=pl.CostEstimate(
            flops=4 * waves * order * len(terms),
            bytes_accessed=nbytes + 4 * waves,
            transcendentals=0,
        ),
    )(*operands)


def local(wavefunction, left_sector, right_sector, left_blocks, right_blocks):
    n_sec = lax.axis_size("sector")
    n_term = lax.axis_size("term")
    order = wavefunction.shape[1]
    held, n_right = right_blocks.shape[:2]
    half = held // 2
    ring = neighbour_ring(n_term)
    sector = lax.axis_index("sector")
    core = sector % 2

    right = jnp.swapaxes(right_blocks, 2, 3).reshape(held * n_right, order, order)
    left = jnp.concatenate(
        [left_blocks] + [from_sector(left_blocks, slot) for slot in range(1, n_sec)], axis=1
    ).reshape(held * n_sec, order, order)
    named = jnp.stack([left_sector[:, 0], right_sector])

    def my_half(blocks):
        n = blocks.shape[0] // 2
        return lax.dynamic_slice_in_dim(blocks, core * n, n)

    totals, waiting = (None, None), [(left, right, half)]
    right_now, left_now = right, left
    for turn in range(1, n_term // 2):
        right_now, left_now = along_ring(right_now, ring), along_ring(left_now, ring)
        if turn == 1:
            sent_named, sent_wave, _ = lax.optimization_barrier((named, wavefunction, right_now))
            sibling_named, sibling_wave = from_sector(sent_named, 1), from_sector(sent_wave, 1)
            table = jnp.stack([
                named[0] ^ sector,
                named[1],
                sibling_named[0] ^ sector,
                sibling_named[1],
                jnp.broadcast_to(core * half, named.shape[1:]),
            ])
        arrived = (left_now, right_now, held)
        if turn > 1 and turn % 2 == 1:
            parts = [(totals[0], wavefunction, 0), (totals[1], sibling_wave, 2)]
            totals = apply_groups(parts, table, waiting[:-1], n_sec, n_right)
            waiting = waiting[-1:]
        left_now, _, totals = lax.optimization_barrier((left_now, right_now, totals))
        waiting.append(arrived)
    far = [(along_ring(my_half(left_now), ring), along_ring(my_half(right_now), ring), half)]
    parts = [(totals[0], wavefunction, 0), (totals[1], sibling_wave, 2)]
    totals = apply_groups(parts, table, waiting, n_sec, n_right)
    (for_sibling,) = apply_groups(
        [(totals[1], sibling_wave, 2)], table, far, n_sec, n_right, jnp.bfloat16
    )
    returned = from_sector(for_sibling, 1)
    (kept,) = apply_groups([(totals[0], wavefunction, 0)], table, far, n_sec, n_right)
    return (kept + returned.astype(jnp.float32)).astype(wavefunction.dtype)


def solution(mesh):
    placed = (
        P(("term", "sector"), None, None),
        P(("term", "sector"), None),
        P(("term", "sector")),
        P("term", "sector", None, None),
        P("term", None, None, None),
    )
    return jax.shard_map(
        local,
        mesh=mesh,
        in_specs=placed,
        out_specs=P(("term", "sector"), None, None),
        check_vma=False,
    )
```

profile of v0, /device:TPU:0, one launch (start us, length us, event | category | flops | bytes accessed | tf_op | source)
XLA Modules:
  0.0 36.9 jit_solution(18022498899127722107)
XLA Ops:
  0.0 0.5 %collective-permute-start.2 = (bf16[2,1,128,128]{3,2,1,0:T(8,128)(2,1)}, bf16[2,1,128,128]{3,2,1,0:T(8,128)(2,1)S(1)}, u32[]{:S(2)}, u32[]{:S(2)}) collective-permute-start(bf16[2,1,128,128]{3,2,1,0:T(8,128)(2,1)} %param.8), channel_id=1, source_target_pairs={{0,1},{1,0},{2,3},{3,2},{4,5},{5,4},{6,7},{7,6},{8,9},{9,8},{10,11... | collective-permute-start | bytes 196616 | tf_op jit(solution)/shard_map/ppermute | solution.py:27
  0.5 2.5 %collective-permute-start.3 = (bf16[2,1,128,128]{3,2,1,0:T(8,128)(2,1)}, bf16[2,1,128,128]{3,2,1,0:T(8,128)(2,1)S(1)}, u32[]{:S(2)}, u32[]{:S(2)}) collective-permute-start(bf16[2,1,128,128]{3,2,1,0:T(8,128)(2,1)} %param.8), channel_id=1, source_target_pairs={{0,2},{1,3},{2,0},{3,1},{4,6},{5,7},{6,4},{7,5},{8,10},{9,11},{10,... | collective-permute-start | bytes 196616 | tf_op jit(solution)/shard_map/ppermute | solution.py:27
  2.9 0.1 collective-permute-start.4
  3.1 0.0 copy-start
  3.1 1.2 %copy.9 = bf16[2,4,128,128]{3,2,1,0:T(8,128)(2,1)S(1)} copy(bf16[2,4,128,128]{2,3,1,0:T(8,128)(2,1)} %bitcast.10) | data formatting | bytes 524288 | tf_op jit(solution)/shard_map/transpose | solution.py:113
  4.3 1.9 %collective-permute-start = (bf16[8,128,128]{2,1,0:T(8,128)(2,1)S(1)}, bf16[8,128,128]{2,1,0:T(8,128)(2,1)S(1)}, u32[]{:S(2)}, u32[]{:S(2)}) collective-permute-start(bf16[8,128,128]{2,1,0:T(8,128)(2,1)S(1)} %bitcast.6), channel_id=1, source_target_pairs={{0,8},{1,5},{2,10},{3,7},{8,16},{9,1},{10,18},{11,3},{16,24},{17,9... | collective-permute-start | bytes 786440 | tf_op jit(solution)/shard_map/ppermute | solution.py:22
  6.1 0.0 collective-permute-done.2
  6.1 0.0 collective-permute-done.3
  6.1 1.1 %collective-permute-done.4 = bf16[2,1,128,128]{3,2,1,0:T(8,128)(2,1)S(1)} collective-permute-done((bf16[2,1,128,128]{3,2,1,0:T(8,128)(2,1)}, bf16[2,1,128,128]{3,2,1,0:T(8,128)(2,1)S(1)}, u32[]{:S(2)}, u32[]{:S(2)}) %collective-permute-start.4) | collective-permute-done | bytes 65568 | tf_op jit(solution)/shard_map/ppermute | solution.py:27
  7.2 0.9 %pad_maximum_fusion = bf16[2,4,128,128]{3,2,1,0:T(8,128)(2,1)S(1)} fusion(bf16[2,1,128,128]{3,2,1,0:T(8,128)(2,1)S(1)} %collective-permute-done.4, bf16[2,1,128,128]{3,2,1,0:T(8,128)(2,1)S(1)} %collective-permute-done.3, bf16[2,1,128,128]{3,2,1,0:T(8,128)(2,1)S(1)} %collective-permute-done.2, bf16[2,1,128,128]{3,2,1,0:T(8,128)(2,1)} %param.8), kind=kLoop, calls=%fused_computation.1 | loop fusion | flops 393216 | bytes 524288 | tf_op jit(solution)/shard_map/concatenate | solution.py:114
  8.1 1.7 %collective-permute-start.5 = (bf16[8,128,128]{2,1,0:T(8,128)(2,1)S(1)}, bf16[8,128,128]{2,1,0:T(8,128)(2,1)S(1)}, u32[]{:S(2)}, u32[]{:S(2)}) collective-permute-start(bf16[8,128,128]{2,1,0:T(8,128)(2,1)S(1)} %bitcast.8), channel_id=1, source_target_pairs={{0,8},{1,5},{2,10},{3,7},{8,16},{9,1},{10,18},{11,3},{16,24},{17,9... | collective-permute-start | bytes 786440 | tf_op jit(solution)/shard_map/ppermute | solution.py:22
  9.8 0.9 %collective-permute-done.refs_4_ = bf16[8,128,128]{2,1,0:T(8,128)(2,1)S(1)} collective-permute-done((bf16[8,128,128]{2,1,0:T(8,128)(2,1)S(1)}, bf16[8,128,128]{2,1,0:T(8,128)(2,1)S(1)}, u32[]{:S(2)}, u32[]{:S(2)}) %collective-permute-start) | collective-permute-done | bytes 262176 | tf_op jit(solution)/shard_map/ppermute | solution.py:22
  10.7 1.8 %collective-permute-start.7 = (bf16[8,128,128]{2,1,0:T(8,128)(2,1)S(1)}, bf16[8,128,128]{2,1,0:T(8,128)(2,1)S(1)}, u32[]{:S(2)}, u32[]{:S(2)}) collective-permute-start(bf16[8,128,128]{2,1,0:T(8,128)(2,1)S(1)} %collective-permute-done.refs_4_), channel_id=1, source_target_pairs={{0,8},{1,5},{2,10},{3,7},{8,16},{9,1},{10,18},{11,3},{16,24},{17,9... | collective-permute-start | bytes 786440 | tf_op jit(solution)/shard_map/ppermute | solution.py:22
  12.5 2.0 %collective-permute-done.5.refs_3_ = bf16[8,128,128]{2,1,0:T(8,128)(2,1)S(1)} collective-permute-done((bf16[8,128,128]{2,1,0:T(8,128)(2,1)S(1)}, bf16[8,128,128]{2,1,0:T(8,128)(2,1)S(1)}, u32[]{:S(2)}, u32[]{:S(2)}) %collective-permute-start.5) | collective-permute-done | bytes 262176 | tf_op jit(solution)/shard_map/ppermute | solution.py:22
  14.5 1.6 %collective-permute-start.6 = (bf16[8,128,128]{2,1,0:T(8,128)(2,1)S(1)}, bf16[8,128,128]{2,1,0:T(8,128)(2,1)S(1)}, u32[]{:S(2)}, u32[]{:S(2)}) collective-permute-start(bf16[8,128,128]{2,1,0:T(8,128)(2,1)S(1)} %collective-permute-done.5.refs_3_), channel_id=1, source_target_pairs={{0,8},{1,5},{2,10},{3,7},{8,16},{9,1},{10,18},{11,3},{16,24},{17,9... | collective-permute-start | bytes 786440 | tf_op jit(solution)/shard_map/ppermute | solution.py:22
  16.2 0.0 copy-start.1
  16.2 0.0 copy-start.2
  16.2 0.7 %copy-done.1 = s32[16]{0:T(128)S(1)} copy-done((s32[16]{0:T(128)S(1)}, s32[16]{0:T(128)}, u32[]{:S(2)}) %copy-start.1) | copy-done | bytes 88
  16.8 0.0 copy-done.2
  16.8 0.0 copy-done
  16.8 0.1 collective-permute-start.10
  16.9 0.4 %collective-permute-done.7.refs_2_ = bf16[8,128,128]{2,1,0:T(8,128)(2,1)S(1)} collective-permute-done((bf16[8,128,128]{2,1,0:T(8,128)(2,1)S(1)}, bf16[8,128,128]{2,1,0:T(8,128)(2,1)S(1)}, u32[]{:S(2)}, u32[]{:S(2)}) %collective-permute-start.7) | collective-permute-done | bytes 262176 | tf_op jit(solution)/shard_map/ppermute | solution.py:22
  17.3 1.6 %collective-permute-start.9 = (bf16[8,128,128]{2,1,0:T(8,128)(2,1)S(1)}, bf16[8,128,128]{2,1,0:T(8,128)(2,1)S(1)}, u32[]{:S(2)}, u32[]{:S(2)}) collective-permute-start(bf16[8,128,128]{2,1,0:T(8,128)(2,1)S(1)} %collective-permute-done.7.refs_2_), channel_id=1, source_target_pairs={{0,8},{1,5},{2,10},{3,7},{8,16},{9,1},{10,18},{11,3},{16,24},{17,9... | collective-permute-start | bytes 786440 | tf_op jit(solution)/shard_map/ppermute | solution.py:22
  19.0 0.0 collective-permute-start.1
  19.0 1.9 %collective-permute-done.6.refs_1_ = bf16[8,128,128]{2,1,0:T(8,128)(2,1)S(1)} collective-permute-done((bf16[8,128,128]{2,1,0:T(8,128)(2,1)S(1)}, bf16[8,128,128]{2,1,0:T(8,128)(2,1)S(1)}, u32[]{:S(2)}, u32[]{:S(2)}) %collective-permute-start.6) | collective-permute-done | bytes 262176 | tf_op jit(solution)/shard_map/ppermute | solution.py:22
  20.9 1.6 %collective-permute-start.8 = (bf16[8,128,128]{2,1,0:T(8,128)(2,1)S(1)}, bf16[8,128,128]{2,1,0:T(8,128)(2,1)S(1)}, u32[]{:S(2)}, u32[]{:S(2)}) collective-permute-start(bf16[8,128,128]{2,1,0:T(8,128)(2,1)S(1)} %collective-permute-done.6.refs_1_), channel_id=1, source_target_pairs={{0,8},{1,5},{2,10},{3,7},{8,16},{9,1},{10,18},{11,3},{16,24},{17,9... | collective-permute-start | bytes 786440 | tf_op jit(solution)/shard_map/ppermute | solution.py:22
  22.5 0.0 collective-permute-done.1
  22.6 1.1 %collective-permute-done.9.refs_4_ = bf16[8,128,128]{2,1,0:T(8,128)(2,1)S(1)} collective-permute-done((bf16[8,128,128]{2,1,0:T(8,128)(2,1)S(1)}, bf16[8,128,128]{2,1,0:T(8,128)(2,1)S(1)}, u32[]{:S(2)}, u32[]{:S(2)}) %collective-permute-start.9) | collective-permute-done | bytes 262176 | tf_op jit(solution)/shard_map/ppermute | solution.py:22
  23.7 1.7 %collective-permute-start.12 = (bf16[4,128,128]{2,1,0:T(8,128)(2,1)S(1)}, bf16[4,128,128]{2,1,0:T(8,128)(2,1)S(1)}, u32[]{:S(2)}, u32[]{:S(2)}) collective-permute-start(bf16[4,128,128]{2,1,0:T(8,128)(2,1)S(1)} %constant_dynamic-slice_fusion), channel_id=1, source_target_pairs={{0,8},{1,5},{2,10},{3,7},{8,16},{9,1},{10,18},{11,3},{16,24},{17,9... | collective-permute-start | bytes 393224 | tf_op jit(solution)/shard_map/ppermute | solution.py:22
  25.4 0.0 collective-permute-done.10.refs_6_.refs_3_
  25.4 2.4 %shard_map.55 = (f32[16,128,128]{2,1,0:T(8,128)S(1)}, f32[16,128,128]{2,1,0:T(8,128)S(1)}) custom-call(s32[5,16]{1,0:T(8,128)S(1)} %stack.13.refs_0_, bf16[8,128,128]{2,1,0:T(8,128)(2,1)S(1)} %bitcast.9, bf16[8,128,128]{2,1,0:T(8,128)(2,1)S(1)} %bitcast.7, bf16[8,128,128]{2,1,0:T(8,128)(2,1)S(1)} %collective-permute-done.5.refs_3_, ...), custom_call_target="tpu_custom_call" | custom-call | flops 805306368 | bytes 4194624 | tf_op jit(solution)/shard_map/pallas_call | solution.py:88
  27.8 0.0 collective-permute-done.8.refs_3_
  27.9 1.6 %collective-permute-start.11 = (bf16[4,128,128]{2,1,0:T(8,128)(2,1)S(1)}, bf16[4,128,128]{2,1,0:T(8,128)(2,1)S(1)}, u32[]{:S(2)}, u32[]{:S(2)}) collective-permute-start(bf16[4,128,128]{2,1,0:T(8,128)(2,1)S(1)} %constant_dynamic-slice_fusion.1), channel_id=1, source_target_pairs={{0,8},{1,5},{2,10},{3,7},{8,16},{9,1},{10,18},{11,3},{16,24},{17,9... | collective-permute-start | bytes 393224 | tf_op jit(solution)/shard_map/ppermute | solution.py:22
  29.5 3.2 %shard_map.56 = (f32[16,128,128]{2,1,0:T(8,128)S(1)}, f32[16,128,128]{2,1,0:T(8,128)S(1)}) custom-call(s32[5,16]{1,0:T(8,128)S(1)} %stack.13.refs_0_, bf16[8,128,128]{2,1,0:T(8,128)(2,1)S(1)} %collective-permute-done.6.refs_1_, bf16[8,128,128]{2,1,0:T(8,128)(2,1)S(1)} %collective-permute-done.7.refs_2_, ...), custom_call_target="tpu_custom_call", output_to_operand_aliasing={{0}: (7, {}), {1}: (8, {})} | custom-call | flops 1073741824 | bytes 6291776 | tf_op jit(solution)/shard_map/pallas_call | solution.py:88
  32.7 0.0 collective-permute-done.12.refs_2_
  32.8 0.1 collective-permute-done.11.refs_1_
  32.9 1.0 %shard_map.58 = bf16[16,128,128]{2,1,0:T(8,128)(2,1)S(1)} custom-call(s32[5,16]{1,0:T(8,128)S(1)} %stack.13.refs_0_, bf16[4,128,128]{2,1,0:T(8,128)(2,1)S(1)} %collective-permute-done.11.refs_1_, bf16[4,128,128]{2,1,0:T(8,128)(2,1)S(1)} %collective-permute-done.12.refs_2_, bf16[16,128,128]{2,1,0:T(8,128)(2,1)S(1)} %collective-permute-done.10.refs_6_.refs_3_, ...), custom_call_target="tpu_custom_call" | custom-call | flops 134217728 | bytes 2883904 | tf_op jit(solution)/shard_map/pallas_call | solution.py:88
  33.9 0.1 collective-permute-start.13
  34.0 1.1 %shard_map.57 = f32[16,128,128]{2,1,0:T(8,128)S(1)} custom-call(s32[5,16]{1,0:T(8,128)S(1)} %stack.13.refs_0_, bf16[4,128,128]{2,1,0:T(8,128)(2,1)S(1)} %collective-permute-done.11.refs_1_, bf16[4,128,128]{2,1,0:T(8,128)(2,1)S(1)} %collective-permute-done.12.refs_2_, bf16[16,128,128]{2,1,0:T(8,128)(2,1)S(1)} %copy-done, ...), custom_call_target="tpu_custom_call", output_to_operand_aliasing={{}: (4, {})} | custom-call | flops 134217728 | bytes 2883904 | tf_op jit(solution)/shard_map/pallas_call | solution.py:88
  35.1 0.8 %collective-permute-done.13 = bf16[16,128,128]{2,1,0:T(8,128)(2,1)S(1)} collective-permute-done((bf16[16,128,128]{2,1,0:T(8,128)(2,1)S(1)}, bf16[16,128,128]{2,1,0:T(8,128)(2,1)S(1)}, u32[]{:S(2)}, u32[]{:S(2)}) %collective-permute-start.13) | collective-permute-done | bytes 524320 | tf_op jit(solution)/shard_map/ppermute | solution.py:27
  35.9 1.0 %add_convert_fusion = bf16[16,128,128]{2,1,0:T(8,128)(2,1)} fusion(f32[16,128,128]{2,1,0:T(8,128)S(1)} %shard_map.57, bf16[16,128,128]{2,1,0:T(8,128)(2,1)S(1)} %collective-permute-done.13), kind=kLoop, calls=%fused_computation | loop fusion | flops 786432 | bytes 2097152 | tf_op jit(solution)/shard_map/convert_element_type | solution.py:152
  (7 shorter events, 0.1 us)
Async XLA Ops:
  0.0 6.1 %collective-permute-start.2 = (bf16[2,1,128,128]{3,2,1,0:T(8,128)(2,1)}, bf16[2,1,128,128]{3,2,1,0:T(8,128)(2,1)S(1)}, u32[]{:S(2)}, u32[]{:S(2)}) collective-permute-start(bf16[2,1,128,128]{3,2,1,0:T(8,128)(2,1)} %param.8), channel_id=1, source_target_pairs={{0,1},{1,0},{2,3},{3,2},{4,5},{5,4},{6,7},{7,6},{8,9},{9,8},{10,11... | collective-permute-start | bytes 196616 | tf_op jit(solution)/shard_map/ppermute | solution.py:27
  0.5 5.7 %collective-permute-start.3 = (bf16[2,1,128,128]{3,2,1,0:T(8,128)(2,1)}, bf16[2,1,128,128]{3,2,1,0:T(8,128)(2,1)S(1)}, u32[]{:S(2)}, u32[]{:S(2)}) collective-permute-start(bf16[2,1,128,128]{3,2,1,0:T(8,128)(2,1)} %param.8), channel_id=1, source_target_pairs={{0,2},{1,3},{2,0},{3,1},{4,6},{5,7},{6,4},{7,5},{8,10},{9,11},{10,... | collective-permute-start | bytes 196616 | tf_op jit(solution)/shard_map/ppermute | solution.py:27
  2.9 4.3 %collective-permute-start.4 = (bf16[2,1,128,128]{3,2,1,0:T(8,128)(2,1)}, bf16[2,1,128,128]{3,2,1,0:T(8,128)(2,1)S(1)}, u32[]{:S(2)}, u32[]{:S(2)}) collective-permute-start(bf16[2,1,128,128]{3,2,1,0:T(8,128)(2,1)} %param.8), channel_id=1, source_target_pairs={{0,3},{1,2},{2,1},{3,0},{4,7},{5,6},{6,5},{7,4},{8,11},{9,10},{10,... | collective-permute-start | bytes 196616 | tf_op jit(solution)/shard_map/ppermute | solution.py:27
  3.1 13.7 %copy-start = (bf16[16,128,128]{2,1,0:T(8,128)(2,1)S(1)}, bf16[16,128,128]{2,1,0:T(8,128)(2,1)}, u32[]{:S(2)}) copy-start(bf16[16,128,128]{2,1,0:T(8,128)(2,1)} %refs_3_.1) | copy-start | bytes 1572868
  4.3 6.4 %collective-permute-start = (bf16[8,128,128]{2,1,0:T(8,128)(2,1)S(1)}, bf16[8,128,128]{2,1,0:T(8,128)(2,1)S(1)}, u32[]{:S(2)}, u32[]{:S(2)}) collective-permute-start(bf16[8,128,128]{2,1,0:T(8,128)(2,1)S(1)} %bitcast.6), channel_id=1, source_target_pairs={{0,8},{1,5},{2,10},{3,7},{8,16},{9,1},{10,18},{11,3},{16,24},{17,9... | collective-permute-start | bytes 786440 | tf_op jit(solution)/shard_map/ppermute | solution.py:22
  8.1 6.4 %collective-permute-start.5 = (bf16[8,128,128]{2,1,0:T(8,128)(2,1)S(1)}, bf16[8,128,128]{2,1,0:T(8,128)(2,1)S(1)}, u32[]{:S(2)}, u32[]{:S(2)}) collective-permute-start(bf16[8,128,128]{2,1,0:T(8,128)(2,1)S(1)} %bitcast.8), channel_id=1, source_target_pairs={{0,8},{1,5},{2,10},{3,7},{8,16},{9,1},{10,18},{11,3},{16,24},{17,9... | collective-permute-start | bytes 786440 | tf_op jit(solution)/shard_map/ppermute | solution.py:22
  10.7 6.6 %collective-permute-start.7 = (bf16[8,128,128]{2,1,0:T(8,128)(2,1)S(1)}, bf16[8,128,128]{2,1,0:T(8,128)(2,1)S(1)}, u32[]{:S(2)}, u32[]{:S(2)}) collective-permute-start(bf16[8,128,128]{2,1,0:T(8,128)(2,1)S(1)} %collective-permute-done.refs_4_), channel_id=1, source_target_pairs={{0,8},{1,5},{2,10},{3,7},{8,16},{9,1},{10,18},{11,3},{16,24},{17,9... | collective-permute-start | bytes 786440 | tf_op jit(solution)/shard_map/ppermute | solution.py:22
  14.5 6.4 %collective-permute-start.6 = (bf16[8,128,128]{2,1,0:T(8,128)(2,1)S(1)}, bf16[8,128,128]{2,1,0:T(8,128)(2,1)S(1)}, u32[]{:S(2)}, u32[]{:S(2)}) collective-permute-start(bf16[8,128,128]{2,1,0:T(8,128)(2,1)S(1)} %collective-permute-done.5.refs_3_), channel_id=1, source_target_pairs={{0,8},{1,5},{2,10},{3,7},{8,16},{9,1},{10,18},{11,3},{16,24},{17,9... | collective-permute-start | bytes 786440 | tf_op jit(solution)/shard_map/ppermute | solution.py:22
  16.2 0.7 %copy-start.1 = (s32[16]{0:T(128)S(1)}, s32[16]{0:T(128)}, u32[]{:S(2)}) copy-start(s32[16]{0:T(128)} %param.7) | copy-start | bytes 196
  16.2 0.7 %copy-start.2 = (s32[16,1]{0,1:T(1,128)S(1)}, s32[16,1]{0,1:T(1,128)}, u32[]{:S(2)}) copy-start(s32[16,1]{0,1:T(1,128)} %param.6) | copy-start | bytes 196
  16.8 8.6 %collective-permute-start.10 = (bf16[16,128,128]{2,1,0:T(8,128)(2,1)S(1)}, bf16[16,128,128]{2,1,0:T(8,128)(2,1)S(1)}, u32[]{:S(2)}, u32[]{:S(2)}) collective-permute-start(bf16[16,128,128]{2,1,0:T(8,128)(2,1)S(1)} %copy-done), channel_id=1, source_target_pairs={{0,1},{1,0},{2,3},{3,2},{4,5},{5,4},{6,7},{7,6},{8,9},{9,8},{10,11... | collective-permute-start | bytes 1572872 | tf_op jit(solution)/shard_map/ppermute | solution.py:27
  17.3 6.4 %collective-permute-start.9 = (bf16[8,128,128]{2,1,0:T(8,128)(2,1)S(1)}, bf16[8,128,128]{2,1,0:T(8,128)(2,1)S(1)}, u32[]{:S(2)}, u32[]{:S(2)}) collective-permute-start(bf16[8,128,128]{2,1,0:T(8,128)(2,1)S(1)} %collective-permute-done.7.refs_2_), channel_id=1, source_target_pairs={{0,8},{1,5},{2,10},{3,7},{8,16},{9,1},{10,18},{11,3},{16,24},{17,9... | collective-permute-start | bytes 786440 | tf_op jit(solution)/shard_map/ppermute | solution.py:22
  19.0 3.6 %collective-permute-start.1 = (s32[2,16]{1,0:T(2,128)S(1)}, s32[2,16]{1,0:T(2,128)S(1)}, u32[]{:S(2)}, u32[]{:S(2)}) collective-permute-start(s32[2,16]{1,0:T(2,128)S(1)} %pad_add_fusion), channel_id=1, source_target_pairs={{0,1},{1,0},{2,3},{3,2},{4,5},{5,4},{6,7},{7,6},{8,9},{9,8},{10,11... | collective-permute-start | bytes 392 | tf_op jit(solution)/shard_map/ppermute | solution.py:27
  20.9 7.0 %collective-permute-start.8 = (bf16[8,128,128]{2,1,0:T(8,128)(2,1)S(1)}, bf16[8,128,128]{2,1,0:T(8,128)(2,1)S(1)}, u32[]{:S(2)}, u32[]{:S(2)}) collective-permute-start(bf16[8,128,128]{2,1,0:T(8,128)(2,1)S(1)} %collective-permute-done.6.refs_1_), channel_id=1, source_target_pairs={{0,8},{1,5},{2,10},{3,7},{8,16},{9,1},{10,18},{11,3},{16,24},{17,9... | collective-permute-start | bytes 786440 | tf_op jit(solution)/shard_map/ppermute | solution.py:22
  23.7 9.0 %collective-permute-start.12 = (bf16[4,128,128]{2,1,0:T(8,128)(2,1)S(1)}, bf16[4,128,128]{2,1,0:T(8,128)(2,1)S(1)}, u32[]{:S(2)}, u32[]{:S(2)}) collective-permute-start(bf16[4,128,128]{2,1,0:T(8,128)(2,1)S(1)} %constant_dynamic-slice_fusion), channel_id=1, source_target_pairs={{0,8},{1,5},{2,10},{3,7},{8,16},{9,1},{10,18},{11,3},{16,24},{17,9... | collective-permute-start | bytes 393224 | tf_op jit(solution)/shard_map/ppermute | solution.py:22
  27.9 5.0 %collective-permute-start.11 = (bf16[4,128,128]{2,1,0:T(8,128)(2,1)S(1)}, bf16[4,128,128]{2,1,0:T(8,128)(2,1)S(1)}, u32[]{:S(2)}, u32[]{:S(2)}) collective-permute-start(bf16[4,128,128]{2,1,0:T(8,128)(2,1)S(1)} %constant_dynamic-slice_fusion.1), channel_id=1, source_target_pairs={{0,8},{1,5},{2,10},{3,7},{8,16},{9,1},{10,18},{11,3},{16,24},{17,9... | collective-permute-start | bytes 393224 | tf_op jit(solution)/shard_map/ppermute | solution.py:22
  33.9 2.0 %collective-permute-start.13 = (bf16[16,128,128]{2,1,0:T(8,128)(2,1)S(1)}, bf16[16,128,128]{2,1,0:T(8,128)(2,1)S(1)}, u32[]{:S(2)}, u32[]{:S(2)}) collective-permute-start(bf16[16,128,128]{2,1,0:T(8,128)(2,1)S(1)} %shard_map.58), channel_id=1, source_target_pairs={{0,1},{1,0},{2,3},{3,2},{4,5},{5,4},{6,7},{7,6},{8,9},{9,8},{10,11... | collective-permute-start | bytes 1572872 | tf_op jit(solution)/shard_map/ppermute | solution.py:27
where the time goes:
time: 37.1 us; the launch traced here: 36.9 us
  starting transfers between devices  16.8 us (45%)
  waiting for transfers between devices  8.51 us (23%)
  Pallas kernels  7.76 us (21%)
  local copies, waits for them, and re-layouts  1.9 us (5%)
  other arithmetic  1.84 us (5%)
    ppermute x8, starting transfers between devices, along_ring(): return lax.ppermute(block, ('term', 'sector'), route)  13.5 us
    pallas_call x4, Pallas kernels, apply_groups(): pl.pallas_call(kernel, out_shape=[jax.ShapeDtypeStruct(part[1].shape, out...  7.76 us
    ppermute x8, waiting for transfers between devices, along_ring(): return lax.ppermute(block, ('term', 'sector'), route)  6.58 us
    ppermute x6, starting transfers between devices, from_sector(): return lax.ppermute(block, 'sector', [(i, i ^ offset) for i in range(n)])  3.23 us
    ppermute x6, waiting for transfers between devices, from_sector(): return lax.ppermute(block, 'sector', [(i, i ^ offset) for i in range(n)])  1.94 us
    transpose x1, local copies, waits for them, and re-layouts, local(): jnp.swapaxes(right_blocks, 2, 3).reshape(held * n_right, order, order)  1.18 us
    convert_element_type x1, other arithmetic, local(): return (kept + returned.astype(jnp.float32)).astype(wavefunction.dtype)  0.95 us
    concatenate x1, other arithmetic, local(): jnp.concatenate([left_blocks] + [from_sector(left_blocks, slot) for slot...  0.87 us
  transfers between devices with their start and end apart: 14, of which 8 were waited for; matrix products, arithmetic and copies ran while one was open for 6% of the time, Pallas kernels for 18%

commit v1 on v0

--- a/solution.py
+++ b/solution.py
@@ -111,9 +111,10 @@
     core = sector % 2
 
     right = jnp.swapaxes(right_blocks, 2, 3).reshape(held * n_right, order, order)
-    left = jnp.concatenate(
-        [left_blocks] + [from_sector(left_blocks, slot) for slot in range(1, n_sec)], axis=1
-    ).reshape(held * n_sec, order, order)
+    pair = jnp.concatenate([left_blocks, from_sector(left_blocks, 1)], axis=1)
+    others = [from_sector(left_blocks, slot) for slot in range(2, n_sec)]
+    pair = lax.optimization_barrier(pair)
+    left = jnp.concatenate([pair] + others, axis=1).reshape(held * n_sec, order, order)
     named = jnp.stack([left_sector[:, 0], right_sector])
 
     def my_half(blocks):
@@ -139,7 +140,9 @@
             parts = [(totals[0], wavefunction, 0), (totals[1], sibling_wave, 2)]
             totals = apply_groups(parts, table, waiting[:-1], n_sec, n_right)
             waiting = waiting[-1:]
-        left_now, _, totals = lax.optimization_barrier((left_now, right_now, totals))
+            right_now, totals = lax.optimization_barrier((right_now, totals))
+        else:
+            left_now, _ = lax.optimization_barrier((left_now, right_now))
         waiting.append(arrived)
     far = [(along_ring(my_half(left_now), ring), along_ring(my_half(right_now), ring), half)]
     parts = [(totals[0], wavefunction, 0), (totals[1], sibling_wave, 2)]

time: 37.1 us -> 35.6 us (0.960)
  other arithmetic: 1.84 us -> 1.01 us
  waiting for transfers between devices: 8.51 us -> 7.8 us
    concatenate x1 -> x2, other arithmetic: 0.87 us -> 0.05 us  [the longest x1 0.03 us: local(): jnp.concatenate([pair] + others, axis=1).reshape(held * n_sec, order, order)]
    ppermute x8, waiting for transfers between devices: 6.58 us -> 5.88 us  [along_ring(): return lax.ppermute(block, ('term', 'sector'), route)]
  transfers between devices with their start and end apart: 14 -> 14, of which waited for: 8 -> 8; matrix products, arithmetic and copies ran while one was open for 6% -> 4% of each run, Pallas kernels for 18% -> 19%
where the time goes in v1:
time: 35.6 us; the launch traced here: 35.4 us
  starting transfers between devices  16.9 us (47%)
  waiting for transfers between devices  7.8 us (22%)
  Pallas kernels  7.76 us (22%)
  local copies, waits for them, and re-layouts  1.88 us (5%)
  other arithmetic  1.01 us (3%)
    ppermute x8, starting transfers between devices, along_ring(): return lax.ppermute(block, ('term', 'sector'), route)  13.7 us
    pallas_call x4, Pallas kernels, apply_groups(): pl.pallas_call(kernel, out_shape=[jax.ShapeDtypeStruct(part[1].shape, out...  7.76 us
    ppermute x8, waiting for transfers between devices, along_ring(): return lax.ppermute(block, ('term', 'sector'), route)  5.88 us
    ppermute x6, starting transfers between devices, from_sector(): return lax.ppermute(block, 'sector', [(i, i ^ offset) for i in range(n)])  3.16 us
    ppermute x6, waiting for transfers between devices, from_sector(): return lax.ppermute(block, 'sector', [(i, i ^ offset) for i in range(n)])  1.92 us
    transpose x1, local copies, waits for them, and re-layouts, local(): jnp.swapaxes(right_blocks, 2, 3).reshape(held * n_right, order, order)  1.15 us
    convert_element_type x1, other arithmetic, local(): return (kept + returned.astype(jnp.float32)).astype(wavefunction.dtype)  0.95 us
  transfers between devices with their start and end apart: 14, of which 8 were waited for; matrix products, arithmetic and copies ran while one was open for 4% of the time, Pallas kernels for 19%

profile of v1, /device:TPU:0, one launch (start us, length us, event | category | flops | bytes accessed | tf_op | source)
XLA Modules:
  0.0 35.4 jit_solution(17013442653758940010)
XLA Ops:
  0.0 0.5 %collective-permute-start.2 = (bf16[2,1,128,128]{3,2,1,0:T(8,128)(2,1)}, bf16[2,1,128,128]{3,2,1,0:T(8,128)(2,1)S(1)}, u32[]{:S(2)}, u32[]{:S(2)}) collective-permute-start(bf16[2,1,128,128]{3,2,1,0:T(8,128)(2,1)} %param.8), channel_id=1, source_target_pairs={{0,1},{1,0},{2,3},{3,2},{4,5},{5,4},{6,7},{7,6},{8,9},{9,8},{10,11... | collective-permute-start | bytes 196616 | tf_op jit(solution)/shard_map/ppermute | solution.py:27
  0.5 2.5 %collective-permute-start.3 = (bf16[2,1,128,128]{3,2,1,0:T(8,128)(2,1)}, bf16[2,1,128,128]{3,2,1,0:T(8,128)(2,1)S(1)}, u32[]{:S(2)}, u32[]{:S(2)}) collective-permute-start(bf16[2,1,128,128]{3,2,1,0:T(8,128)(2,1)} %param.8), channel_id=1, source_target_pairs={{0,2},{1,3},{2,0},{3,1},{4,6},{5,7},{6,4},{7,5},{8,10},{9,11},{10,... | collective-permute-start | bytes 196616 | tf_op jit(solution)/shard_map/ppermute | solution.py:27
  2.9 0.1 collective-permute-start.4
  3.1 0.0 copy-start.1
  3.1 1.1 %copy.9 = bf16[2,4,128,128]{3,2,1,0:T(8,128)(2,1)S(1)} copy(bf16[2,4,128,128]{2,3,1,0:T(8,128)(2,1)} %bitcast.10) | data formatting | bytes 524288 | tf_op jit(solution)/shard_map/transpose | solution.py:113
  4.2 0.0 copy-start
  4.3 1.9 %collective-permute-start = (bf16[8,128,128]{2,1,0:T(8,128)(2,1)S(1)}, bf16[8,128,128]{2,1,0:T(8,128)(2,1)S(1)}, u32[]{:S(2)}, u32[]{:S(2)}) collective-permute-start(bf16[8,128,128]{2,1,0:T(8,128)(2,1)S(1)} %bitcast.6), channel_id=1, source_target_pairs={{0,8},{1,5},{2,10},{3,7},{8,16},{9,1},{10,18},{11,3},{16,24},{17,9... | collective-permute-start | bytes 786440 | tf_op jit(solution)/shard_map/ppermute | solution.py:22
  6.1 0.0 collective-permute-done.2
  6.1 0.0 copy-done.1
  6.1 0.0 collective-permute-done.3
  6.1 1.1 %collective-permute-done.4 = bf16[2,1,128,128]{3,2,1,0:T(8,128)(2,1)S(1)} collective-permute-done((bf16[2,1,128,128]{3,2,1,0:T(8,128)(2,1)}, bf16[2,1,128,128]{3,2,1,0:T(8,128)(2,1)S(1)}, u32[]{:S(2)}, u32[]{:S(2)}) %collective-permute-start.4) | collective-permute-done | bytes 65568 | tf_op jit(solution)/shard_map/ppermute | solution.py:27
  7.3 1.7 %collective-permute-start.5 = (bf16[8,128,128]{2,1,0:T(8,128)(2,1)S(1)}, bf16[8,128,128]{2,1,0:T(8,128)(2,1)S(1)}, u32[]{:S(2)}, u32[]{:S(2)}) collective-permute-start(bf16[8,128,128]{2,1,0:T(8,128)(2,1)S(1)} %bitcast.8), channel_id=1, source_target_pairs={{0,8},{1,5},{2,10},{3,7},{8,16},{9,1},{10,18},{11,3},{16,24},{17,9... | collective-permute-start | bytes 786440 | tf_op jit(solution)/shard_map/ppermute | solution.py:22
  8.9 0.0 copy-start.2
  8.9 0.0 copy-start.3
  8.9 0.7 %copy-done.2 = s32[16]{0:T(128)S(1)} copy-done((s32[16]{0:T(128)S(1)}, s32[16]{0:T(128)}, u32[]{:S(2)}) %copy-start.2) | copy-done | bytes 88
  9.6 0.0 copy-done.3
  9.6 1.1 %collective-permute-done.refs_4_ = bf16[8,128,128]{2,1,0:T(8,128)(2,1)S(1)} collective-permute-done((bf16[8,128,128]{2,1,0:T(8,128)(2,1)S(1)}, bf16[8,128,128]{2,1,0:T(8,128)(2,1)S(1)}, u32[]{:S(2)}, u32[]{:S(2)}) %collective-permute-start) | collective-permute-done | bytes 262176 | tf_op jit(solution)/shard_map/ppermute | solution.py:22
  10.7 0.0 copy-done
  10.7 0.0 collective-permute-start.11
  10.7 1.8 %collective-permute-start.7 = (bf16[8,128,128]{2,1,0:T(8,128)(2,1)S(1)}, bf16[8,128,128]{2,1,0:T(8,128)(2,1)S(1)}, u32[]{:S(2)}, u32[]{:S(2)}) collective-permute-start(bf16[8,128,128]{2,1,0:T(8,128)(2,1)S(1)} %collective-permute-done.refs_4_), channel_id=1, source_target_pairs={{0,8},{1,5},{2,10},{3,7},{8,16},{9,1},{10,18},{11,3},{16,24},{17,9... | collective-permute-start | bytes 786440 | tf_op jit(solution)/shard_map/ppermute | solution.py:22
  12.5 1.2 %collective-permute-done.5.refs_3_ = bf16[8,128,128]{2,1,0:T(8,128)(2,1)S(1)} collective-permute-done((bf16[8,128,128]{2,1,0:T(8,128)(2,1)S(1)}, bf16[8,128,128]{2,1,0:T(8,128)(2,1)S(1)}, u32[]{:S(2)}, u32[]{:S(2)}) %collective-permute-start.5) | collective-permute-done | bytes 262176 | tf_op jit(solution)/shard_map/ppermute | solution.py:22
  13.7 1.6 %collective-permute-start.6 = (bf16[8,128,128]{2,1,0:T(8,128)(2,1)S(1)}, bf16[8,128,128]{2,1,0:T(8,128)(2,1)S(1)}, u32[]{:S(2)}, u32[]{:S(2)}) collective-permute-start(bf16[8,128,128]{2,1,0:T(8,128)(2,1)S(1)} %collective-permute-done.5.refs_3_), channel_id=1, source_target_pairs={{0,8},{1,5},{2,10},{3,7},{8,16},{9,1},{10,18},{11,3},{16,24},{17,9... | collective-permute-start | bytes 786440 | tf_op jit(solution)/shard_map/ppermute | solution.py:22
  15.3 0.0 collective-permute-start.1
  15.3 1.7 %collective-permute-done.7.refs_2_ = bf16[8,128,128]{2,1,0:T(8,128)(2,1)S(1)} collective-permute-done((bf16[8,128,128]{2,1,0:T(8,128)(2,1)S(1)}, bf16[8,128,128]{2,1,0:T(8,128)(2,1)S(1)}, u32[]{:S(2)}, u32[]{:S(2)}) %collective-permute-start.7) | collective-permute-done | bytes 262176 | tf_op jit(solution)/shard_map/ppermute | solution.py:22
  17.1 1.8 %collective-permute-start.10 = (bf16[8,128,128]{2,1,0:T(8,128)(2,1)S(1)}, bf16[8,128,128]{2,1,0:T(8,128)(2,1)S(1)}, u32[]{:S(2)}, u32[]{:S(2)}) collective-permute-start(bf16[8,128,128]{2,1,0:T(8,128)(2,1)S(1)} %collective-permute-done.7.refs_2_), channel_id=1, source_target_pairs={{0,8},{1,5},{2,10},{3,7},{8,16},{9,1},{10,18},{11,3},{16,24},{17,9... | collective-permute-start | bytes 786440 | tf_op jit(solution)/shard_map/ppermute | solution.py:22
  18.9 1.2 %collective-permute-done.6.refs_1_ = bf16[8,128,128]{2,1,0:T(8,128)(2,1)S(1)} collective-permute-done((bf16[8,128,128]{2,1,0:T(8,128)(2,1)S(1)}, bf16[8,128,128]{2,1,0:T(8,128)(2,1)S(1)}, u32[]{:S(2)}, u32[]{:S(2)}) %collective-permute-start.6) | collective-permute-done | bytes 262176 | tf_op jit(solution)/shard_map/ppermute | solution.py:22
  20.1 1.6 %collective-permute-start.8 = (bf16[8,128,128]{2,1,0:T(8,128)(2,1)S(1)}, bf16[8,128,128]{2,1,0:T(8,128)(2,1)S(1)}, u32[]{:S(2)}, u32[]{:S(2)}) collective-permute-start(bf16[8,128,128]{2,1,0:T(8,128)(2,1)S(1)} %collective-permute-done.6.refs_1_), channel_id=1, source_target_pairs={{0,8},{1,5},{2,10},{3,7},{8,16},{9,1},{10,18},{11,3},{16,24},{17,9... | collective-permute-start | bytes 786440 | tf_op jit(solution)/shard_map/ppermute | solution.py:22
  21.7 0.0 collective-permute-done.1
  21.7 0.0 collective-permute-done.11.refs_6_.refs_3_
  21.7 2.4 %shard_map.55 = (f32[16,128,128]{2,1,0:T(8,128)S(1)}, f32[16,128,128]{2,1,0:T(8,128)S(1)}) custom-call(s32[5,16]{1,0:T(8,128)S(1)} %stack.13.refs_0_, bf16[8,128,128]{2,1,0:T(8,128)(2,1)S(1)} %bitcast.9, bf16[8,128,128]{2,1,0:T(8,128)(2,1)S(1)} %bitcast.7, bf16[8,128,128]{2,1,0:T(8,128)(2,1)S(1)} %collective-permute-done.5.refs_3_, ...), custom_call_target="tpu_custom_call" | custom-call | flops 805306368 | bytes 4194624 | tf_op jit(solution)/shard_map/pallas_call | solution.py:88
  24.2 0.0 collective-permute-done.10.refs_4_
  24.2 1.6 %collective-permute-start.12 = (bf16[4,128,128]{2,1,0:T(8,128)(2,1)S(1)}, bf16[4,128,128]{2,1,0:T(8,128)(2,1)S(1)}, u32[]{:S(2)}, u32[]{:S(2)}) collective-permute-start(bf16[4,128,128]{2,1,0:T(8,128)(2,1)S(1)} %constant_dynamic-slice_fusion), channel_id=1, source_target_pairs={{0,8},{1,5},{2,10},{3,7},{8,16},{9,1},{10,18},{11,3},{16,24},{17,9... | collective-permute-start | bytes 393224 | tf_op jit(solution)/shard_map/ppermute | solution.py:22
  25.8 0.6 %collective-permute-done.8.refs_3_ = bf16[8,128,128]{2,1,0:T(8,128)(2,1)S(1)} collective-permute-done((bf16[8,128,128]{2,1,0:T(8,128)(2,1)S(1)}, bf16[8,128,128]{2,1,0:T(8,128)(2,1)S(1)}, u32[]{:S(2)}, u32[]{:S(2)}) %collective-permute-start.8) | collective-permute-done | bytes 262176 | tf_op jit(solution)/shard_map/ppermute | solution.py:22
  26.4 1.7 %collective-permute-start.9 = (bf16[4,128,128]{2,1,0:T(8,128)(2,1)S(1)}, bf16[4,128,128]{2,1,0:T(8,128)(2,1)S(1)}, u32[]{:S(2)}, u32[]{:S(2)}) collective-permute-start(bf16[4,128,128]{2,1,0:T(8,128)(2,1)S(1)} %constant_dynamic-slice_fusion.1), channel_id=1, source_target_pairs={{0,8},{1,5},{2,10},{3,7},{8,16},{9,1},{10,18},{11,3},{16,24},{17,9... | collective-permute-start | bytes 393224 | tf_op jit(solution)/shard_map/ppermute | solution.py:22
  28.1 3.2 %shard_map.56 = (f32[16,128,128]{2,1,0:T(8,128)S(1)}, f32[16,128,128]{2,1,0:T(8,128)S(1)}) custom-call(s32[5,16]{1,0:T(8,128)S(1)} %stack.13.refs_0_, bf16[8,128,128]{2,1,0:T(8,128)(2,1)S(1)} %collective-permute-done.6.refs_1_, bf16[8,128,128]{2,1,0:T(8,128)(2,1)S(1)} %collective-permute-done.7.refs_2_, ...), custom_call_target="tpu_custom_call", output_to_operand_aliasing={{0}: (7, {}), {1}: (8, {})} | custom-call | flops 1073741824 | bytes 6291776 | tf_op jit(solution)/shard_map/pallas_call | solution.py:88
  31.4 0.0 collective-permute-done.12.refs_2_
  31.4 0.1 collective-permute-done.9.refs_1_
  31.5 1.0 %shard_map.58 = bf16[16,128,128]{2,1,0:T(8,128)(2,1)S(1)} custom-call(s32[5,16]{1,0:T(8,128)S(1)} %stack.13.refs_0_, bf16[4,128,128]{2,1,0:T(8,128)(2,1)S(1)} %collective-permute-done.9.refs_1_, bf16[4,128,128]{2,1,0:T(8,128)(2,1)S(1)} %collective-permute-done.12.refs_2_, bf16[16,128,128]{2,1,0:T(8,128)(2,1)S(1)} %collective-permute-done.11.refs_6_.refs_3_, ...), custom_call_target="tpu_custom_call" | custom-call | flops 134217728 | bytes 2883904 | tf_op jit(solution)/shard_map/pallas_call | solution.py:88
  32.5 0.1 collective-permute-start.13
  32.6 1.1 %shard_map.57 = f32[16,128,128]{2,1,0:T(8,128)S(1)} custom-call(s32[5,16]{1,0:T(8,128)S(1)} %stack.13.refs_0_, bf16[4,128,128]{2,1,0:T(8,128)(2,1)S(1)} %collective-permute-done.9.refs_1_, bf16[4,128,128]{2,1,0:T(8,128)(2,1)S(1)} %collective-permute-done.12.refs_2_, bf16[16,128,128]{2,1,0:T(8,128)(2,1)S(1)} %copy-done, ...), custom_call_target="tpu_custom_call", output_to_operand_aliasing={{}: (4, {})} | custom-call | flops 134217728 | bytes 2883904 | tf_op jit(solution)/shard_map/pallas_call | solution.py:88
  33.6 0.8 %collective-permute-done.13 = bf16[16,128,128]{2,1,0:T(8,128)(2,1)S(1)} collective-permute-done((bf16[16,128,128]{2,1,0:T(8,128)(2,1)S(1)}, bf16[16,128,128]{2,1,0:T(8,128)(2,1)S(1)}, u32[]{:S(2)}, u32[]{:S(2)}) %collective-permute-start.13) | collective-permute-done | bytes 524320 | tf_op jit(solution)/shard_map/ppermute | solution.py:27
  34.5 1.0 %add_convert_fusion = bf16[16,128,128]{2,1,0:T(8,128)(2,1)} fusion(f32[16,128,128]{2,1,0:T(8,128)S(1)} %shard_map.57, bf16[16,128,128]{2,1,0:T(8,128)(2,1)S(1)} %collective-permute-done.13), kind=kLoop, calls=%fused_computation | loop fusion | flops 786432 | bytes 2097152 | tf_op jit(solution)/shard_map/convert_element_type | solution.py:155
  (9 shorter events, 0.1 us)
Async XLA Ops:
  0.0 6.1 %collective-permute-start.2 = (bf16[2,1,128,128]{3,2,1,0:T(8,128)(2,1)}, bf16[2,1,128,128]{3,2,1,0:T(8,128)(2,1)S(1)}, u32[]{:S(2)}, u32[]{:S(2)}) collective-permute-start(bf16[2,1,128,128]{3,2,1,0:T(8,128)(2,1)} %param.8), channel_id=1, source_target_pairs={{0,1},{1,0},{2,3},{3,2},{4,5},{5,4},{6,7},{7,6},{8,9},{9,8},{10,11... | collective-permute-start | bytes 196616 | tf_op jit(solution)/shard_map/ppermute | solution.py:27
  0.5 5.7 %collective-permute-start.3 = (bf16[2,1,128,128]{3,2,1,0:T(8,128)(2,1)}, bf16[2,1,128,128]{3,2,1,0:T(8,128)(2,1)S(1)}, u32[]{:S(2)}, u32[]{:S(2)}) collective-permute-start(bf16[2,1,128,128]{3,2,1,0:T(8,128)(2,1)} %param.8), channel_id=1, source_target_pairs={{0,2},{1,3},{2,0},{3,1},{4,6},{5,7},{6,4},{7,5},{8,10},{9,11},{10,... | collective-permute-start | bytes 196616 | tf_op jit(solution)/shard_map/ppermute | solution.py:27
  2.9 4.3 %collective-permute-start.4 = (bf16[2,1,128,128]{3,2,1,0:T(8,128)(2,1)}, bf16[2,1,128,128]{3,2,1,0:T(8,128)(2,1)S(1)}, u32[]{:S(2)}, u32[]{:S(2)}) collective-permute-start(bf16[2,1,128,128]{3,2,1,0:T(8,128)(2,1)} %param.8), channel_id=1, source_target_pairs={{0,3},{1,2},{2,1},{3,0},{4,7},{5,6},{6,5},{7,4},{8,11},{9,10},{10,... | collective-permute-start | bytes 196616 | tf_op jit(solution)/shard_map/ppermute | solution.py:27
  3.1 3.0 %copy-start.1 = (bf16[2,1,128,128]{3,2,1,0:T(8,128)(2,1)S(1)}, bf16[2,1,128,128]{3,2,1,0:T(8,128)(2,1)}, u32[]{:S(2)}) copy-start(bf16[2,1,128,128]{3,2,1,0:T(8,128)(2,1)} %param.8) | copy-start | bytes 196612
  4.2 6.4 %copy-start = (bf16[16,128,128]{2,1,0:T(8,128)(2,1)S(1)}, bf16[16,128,128]{2,1,0:T(8,128)(2,1)}, u32[]{:S(2)}) copy-start(bf16[16,128,128]{2,1,0:T(8,128)(2,1)} %refs_3_.1) | copy-start | bytes 1572868
  4.3 6.4 %collective-permute-start = (bf16[8,128,128]{2,1,0:T(8,128)(2,1)S(1)}, bf16[8,128,128]{2,1,0:T(8,128)(2,1)S(1)}, u32[]{:S(2)}, u32[]{:S(2)}) collective-permute-start(bf16[8,128,128]{2,1,0:T(8,128)(2,1)S(1)} %bitcast.6), channel_id=1, source_target_pairs={{0,8},{1,5},{2,10},{3,7},{8,16},{9,1},{10,18},{11,3},{16,24},{17,9... | collective-permute-start | bytes 786440 | tf_op jit(solution)/shard_map/ppermute | solution.py:22
  7.3 6.4 %collective-permute-start.5 = (bf16[8,128,128]{2,1,0:T(8,128)(2,1)S(1)}, bf16[8,128,128]{2,1,0:T(8,128)(2,1)S(1)}, u32[]{:S(2)}, u32[]{:S(2)}) collective-permute-start(bf16[8,128,128]{2,1,0:T(8,128)(2,1)S(1)} %bitcast.8), channel_id=1, source_target_pairs={{0,8},{1,5},{2,10},{3,7},{8,16},{9,1},{10,18},{11,3},{16,24},{17,9... | collective-permute-start | bytes 786440 | tf_op jit(solution)/shard_map/ppermute | solution.py:22
  8.9 0.7 %copy-start.2 = (s32[16]{0:T(128)S(1)}, s32[16]{0:T(128)}, u32[]{:S(2)}) copy-start(s32[16]{0:T(128)} %param.7) | copy-start | bytes 196
  8.9 0.7 %copy-start.3 = (s32[16,1]{0,1:T(1,128)S(1)}, s32[16,1]{0,1:T(1,128)}, u32[]{:S(2)}) copy-start(s32[16,1]{0,1:T(1,128)} %param.6) | copy-start | bytes 196
  10.7 11.0 %collective-permute-start.11 = (bf16[16,128,128]{2,1,0:T(8,128)(2,1)S(1)}, bf16[16,128,128]{2,1,0:T(8,128)(2,1)S(1)}, u32[]{:S(2)}, u32[]{:S(2)}) collective-permute-start(bf16[16,128,128]{2,1,0:T(8,128)(2,1)S(1)} %copy-done), channel_id=1, source_target_pairs={{0,1},{1,0},{2,3},{3,2},{4,5},{5,4},{6,7},{7,6},{8,9},{9,8},{10,11... | collective-permute-start | bytes 1572872 | tf_op jit(solution)/shard_map/ppermute | solution.py:27
  10.7 6.4 %collective-permute-start.7 = (bf16[8,128,128]{2,1,0:T(8,128)(2,1)S(1)}, bf16[8,128,128]{2,1,0:T(8,128)(2,1)S(1)}, u32[]{:S(2)}, u32[]{:S(2)}) collective-permute-start(bf16[8,128,128]{2,1,0:T(8,128)(2,1)S(1)} %collective-permute-done.refs_4_), channel_id=1, source_target_pairs={{0,8},{1,5},{2,10},{3,7},{8,16},{9,1},{10,18},{11,3},{16,24},{17,9... | collective-permute-start | bytes 786440 | tf_op jit(solution)/shard_map/ppermute | solution.py:22
  13.7 6.4 %collective-permute-start.6 = (bf16[8,128,128]{2,1,0:T(8,128)(2,1)S(1)}, bf16[8,128,128]{2,1,0:T(8,128)(2,1)S(1)}, u32[]{:S(2)}, u32[]{:S(2)}) collective-permute-start(bf16[8,128,128]{2,1,0:T(8,128)(2,1)S(1)} %collective-permute-done.5.refs_3_), channel_id=1, source_target_pairs={{0,8},{1,5},{2,10},{3,7},{8,16},{9,1},{10,18},{11,3},{16,24},{17,9... | collective-permute-start | bytes 786440 | tf_op jit(solution)/shard_map/ppermute | solution.py:22
  15.3 6.4 %collective-permute-start.1 = (s32[2,16]{1,0:T(2,128)S(1)}, s32[2,16]{1,0:T(2,128)S(1)}, u32[]{:S(2)}, u32[]{:S(2)}) collective-permute-start(s32[2,16]{1,0:T(2,128)S(1)} %pad_add_fusion), channel_id=1, source_target_pairs={{0,1},{1,0},{2,3},{3,2},{4,5},{5,4},{6,7},{7,6},{8,9},{9,8},{10,11... | collective-permute-start | bytes 392 | tf_op jit(solution)/shard_map/ppermute | solution.py:27
  17.1 7.1 %collective-permute-start.10 = (bf16[8,128,128]{2,1,0:T(8,128)(2,1)S(1)}, bf16[8,128,128]{2,1,0:T(8,128)(2,1)S(1)}, u32[]{:S(2)}, u32[]{:S(2)}) collective-permute-start(bf16[8,128,128]{2,1,0:T(8,128)(2,1)S(1)} %collective-permute-done.7.refs_2_), channel_id=1, source_target_pairs={{0,8},{1,5},{2,10},{3,7},{8,16},{9,1},{10,18},{11,3},{16,24},{17,9... | collective-permute-start | bytes 786440 | tf_op jit(solution)/shard_map/ppermute | solution.py:22
  20.1 6.4 %collective-permute-start.8 = (bf16[8,128,128]{2,1,0:T(8,128)(2,1)S(1)}, bf16[8,128,128]{2,1,0:T(8,128)(2,1)S(1)}, u32[]{:S(2)}, u32[]{:S(2)}) collective-permute-start(bf16[8,128,128]{2,1,0:T(8,128)(2,1)S(1)} %collective-permute-done.6.refs_1_), channel_id=1, source_target_pairs={{0,8},{1,5},{2,10},{3,7},{8,16},{9,1},{10,18},{11,3},{16,24},{17,9... | collective-permute-start | bytes 786440 | tf_op jit(solution)/shard_map/ppermute | solution.py:22
  24.2 7.2 %collective-permute-start.12 = (bf16[4,128,128]{2,1,0:T(8,128)(2,1)S(1)}, bf16[4,128,128]{2,1,0:T(8,128)(2,1)S(1)}, u32[]{:S(2)}, u32[]{:S(2)}) collective-permute-start(bf16[4,128,128]{2,1,0:T(8,128)(2,1)S(1)} %constant_dynamic-slice_fusion), channel_id=1, source_target_pairs={{0,8},{1,5},{2,10},{3,7},{8,16},{9,1},{10,18},{11,3},{16,24},{17,9... | collective-permute-start | bytes 393224 | tf_op jit(solution)/shard_map/ppermute | solution.py:22
  26.4 5.0 %collective-permute-start.9 = (bf16[4,128,128]{2,1,0:T(8,128)(2,1)S(1)}, bf16[4,128,128]{2,1,0:T(8,128)(2,1)S(1)}, u32[]{:S(2)}, u32[]{:S(2)}) collective-permute-start(bf16[4,128,128]{2,1,0:T(8,128)(2,1)S(1)} %constant_dynamic-slice_fusion.1), channel_id=1, source_target_pairs={{0,8},{1,5},{2,10},{3,7},{8,16},{9,1},{10,18},{11,3},{16,24},{17,9... | collective-permute-start | bytes 393224 | tf_op jit(solution)/shard_map/ppermute | solution.py:22
  32.5 2.0 %collective-permute-start.13 = (bf16[16,128,128]{2,1,0:T(8,128)(2,1)S(1)}, bf16[16,128,128]{2,1,0:T(8,128)(2,1)S(1)}, u32[]{:S(2)}, u32[]{:S(2)}) collective-permute-start(bf16[16,128,128]{2,1,0:T(8,128)(2,1)S(1)} %shard_map.58), channel_id=1, source_target_pairs={{0,1},{1,0},{2,3},{3,2},{4,5},{5,4},{6,7},{7,6},{8,9},{9,8},{10,11... | collective-permute-start | bytes 1572872 | tf_op jit(solution)/shard_map/ppermute | solution.py:27

commit v2 on v1

--- a/solution.py
+++ b/solution.py
@@ -111,10 +111,12 @@
     core = sector % 2
 
     right = jnp.swapaxes(right_blocks, 2, 3).reshape(held * n_right, order, order)
-    pair = jnp.concatenate([left_blocks, from_sector(left_blocks, 1)], axis=1)
-    others = [from_sector(left_blocks, slot) for slot in range(2, n_sec)]
-    pair = lax.optimization_barrier(pair)
-    left = jnp.concatenate([pair] + others, axis=1).reshape(held * n_sec, order, order)
+    far_slots = jnp.concatenate([from_sector(left_blocks, slot) for slot in range(2, n_sec)], axis=1)
+    far_slots = lax.optimization_barrier(far_slots)
+    room = ((0, 0), (0, n_sec - 1), (0, 0), (0, 0))
+    laid_out = lax.optimization_barrier(jnp.pad(left_blocks, room))
+    left = jnp.concatenate([laid_out[:, :1], from_sector(left_blocks, 1), far_slots], axis=1)
+    left = left.reshape(held * n_sec, order, order)
     named = jnp.stack([left_sector[:, 0], right_sector])
 
     def my_half(blocks):

time: 35.6 us -> 35.7 us (level)
  starting transfers between devices: 16.9 us -> 18.2 us
  waiting for transfers between devices: 7.8 us -> 6.57 us
    ppermute x8, starting transfers between devices: 13.7 us -> 15 us  [along_ring(): return lax.ppermute(block, ('term', 'sector'), route)]
    ppermute x8, waiting for transfers between devices: 5.88 us -> 4.9 us  [along_ring(): return lax.ppermute(block, ('term', 'sector'), route)]
  transfers between devices with their start and end apart: 14 -> 14, of which waited for: 8 -> 7; matrix products, arithmetic and copies ran while one was open for 4% -> 4% of each run, Pallas kernels for 19% -> 19%
where the time goes in v2:
time: 35.7 us; the launch traced here: 35.6 us
  starting transfers between devices  18.2 us (51%)
  Pallas kernels  7.76 us (22%)
  waiting for transfers between devices  6.57 us (18%)
  local copies, waits for them, and re-layouts  1.92 us (5%)
  other arithmetic  1.01 us (3%)
    ppermute x8, starting transfers between devices, along_ring(): return lax.ppermute(block, ('term', 'sector'), route)  15 us
    pallas_call x4, Pallas kernels, apply_groups(): pl.pallas_call(kernel, out_shape=[jax.ShapeDtypeStruct(part[1].shape, out...  7.76 us
    ppermute x8, waiting for transfers between devices, along_ring(): return lax.ppermute(block, ('term', 'sector'), route)  4.9 us
    ppermute x6, starting transfers between devices, from_sector(): return lax.ppermute(block, 'sector', [(i, i ^ offset) for i in range(n)])  3.16 us
    ppermute x6, waiting for transfers between devices, from_sector(): return lax.ppermute(block, 'sector', [(i, i ^ offset) for i in range(n)])  1.67 us
    transpose x1, local copies, waits for them, and re-layouts, local(): jnp.swapaxes(right_blocks, 2, 3).reshape(held * n_right, order, order)  1.15 us
    convert_element_type x1, other arithmetic, local(): return (kept + returned.astype(jnp.float32)).astype(wavefunction.dtype)  0.95 us
  transfers between devices with their start and end apart: 14, of which 7 were waited for; matrix products, arithmetic and copies ran while one was open for 4% of the time, Pallas kernels for 19%

profile of v2, /device:TPU:0, one launch (start us, length us, event | category | flops | bytes accessed | tf_op | source)
XLA Modules:
  0.0 35.6 jit_solution(5145034457776010766)
XLA Ops:
  0.0 2.9 %collective-permute-start.3 = (bf16[2,1,128,128]{3,2,1,0:T(8,128)(2,1)}, bf16[2,1,128,128]{3,2,1,0:T(8,128)(2,1)S(1)}, u32[]{:S(2)}, u32[]{:S(2)}) collective-permute-start(bf16[2,1,128,128]{3,2,1,0:T(8,128)(2,1)} %param.8), channel_id=1, source_target_pairs={{0,2},{1,3},{2,0},{3,1},{4,6},{5,7},{6,4},{7,5},{8,10},{9,11},{10,... | collective-permute-start | bytes 196616 | tf_op jit(solution)/shard_map/ppermute | solution.py:27
  2.9 0.0 collective-permute-start.4
  2.9 0.1 collective-permute-start.2
  3.1 0.0 copy-start.1
  3.1 1.1 %copy.9 = bf16[2,4,128,128]{3,2,1,0:T(8,128)(2,1)S(1)} copy(bf16[2,4,128,128]{2,3,1,0:T(8,128)(2,1)} %bitcast.10) | data formatting | bytes 524288 | tf_op jit(solution)/shard_map/transpose | solution.py:113
  4.2 2.1 %collective-permute-start = (bf16[8,128,128]{2,1,0:T(8,128)(2,1)S(1)}, bf16[8,128,128]{2,1,0:T(8,128)(2,1)S(1)}, u32[]{:S(2)}, u32[]{:S(2)}) collective-permute-start(bf16[8,128,128]{2,1,0:T(8,128)(2,1)S(1)} %bitcast.6), channel_id=1, source_target_pairs={{0,8},{1,5},{2,10},{3,7},{8,16},{9,1},{10,18},{11,3},{16,24},{17,9... | collective-permute-start | bytes 786440 | tf_op jit(solution)/shard_map/ppermute | solution.py:22
  6.4 0.0 copy-done.1
  6.4 0.0 copy-start
  6.4 0.0 collective-permute-done.3
  6.5 0.8 %collective-permute-done.4 = bf16[2,1,128,128]{3,2,1,0:T(8,128)(2,1)S(1)} collective-permute-done((bf16[2,1,128,128]{3,2,1,0:T(8,128)(2,1)}, bf16[2,1,128,128]{3,2,1,0:T(8,128)(2,1)S(1)}, u32[]{:S(2)}, u32[]{:S(2)}) %collective-permute-start.4) | collective-permute-done | bytes 65568 | tf_op jit(solution)/shard_map/ppermute | solution.py:27
  7.3 0.0 collective-permute-done.2
  7.3 1.7 %collective-permute-start.5 = (bf16[8,128,128]{2,1,0:T(8,128)(2,1)S(1)}, bf16[8,128,128]{2,1,0:T(8,128)(2,1)S(1)}, u32[]{:S(2)}, u32[]{:S(2)}) collective-permute-start(bf16[8,128,128]{2,1,0:T(8,128)(2,1)S(1)} %bitcast.8), channel_id=1, source_target_pairs={{0,8},{1,5},{2,10},{3,7},{8,16},{9,1},{10,18},{11,3},{16,24},{17,9... | collective-permute-start | bytes 786440 | tf_op jit(solution)/shard_map/ppermute | solution.py:22
  9.0 0.0 copy-start.2
  9.0 0.0 copy-start.3
  9.0 0.7 %copy-done.2 = s32[16]{0:T(128)S(1)} copy-done((s32[16]{0:T(128)S(1)}, s32[16]{0:T(128)}, u32[]{:S(2)}) %copy-start.2) | copy-done | bytes 88
  9.7 0.0 copy-done.3
  9.7 1.0 %collective-permute-done.refs_4_ = bf16[8,128,128]{2,1,0:T(8,128)(2,1)S(1)} collective-permute-done((bf16[8,128,128]{2,1,0:T(8,128)(2,1)S(1)}, bf16[8,128,128]{2,1,0:T(8,128)(2,1)S(1)}, u32[]{:S(2)}, u32[]{:S(2)}) %collective-permute-start) | collective-permute-done | bytes 262176 | tf_op jit(solution)/shard_map/ppermute | solution.py:22
  10.7 0.0 copy-done
  10.7 0.0 collective-permute-start.11
  10.7 2.1 %collective-permute-start.7 = (bf16[8,128,128]{2,1,0:T(8,128)(2,1)S(1)}, bf16[8,128,128]{2,1,0:T(8,128)(2,1)S(1)}, u32[]{:S(2)}, u32[]{:S(2)}) collective-permute-start(bf16[8,128,128]{2,1,0:T(8,128)(2,1)S(1)} %collective-permute-done.refs_4_), channel_id=1, source_target_pairs={{0,8},{1,5},{2,10},{3,7},{8,16},{9,1},{10,18},{11,3},{16,24},{17,9... | collective-permute-start | bytes 786440 | tf_op jit(solution)/shard_map/ppermute | solution.py:22
  12.8 1.0 %collective-permute-done.5.refs_3_ = bf16[8,128,128]{2,1,0:T(8,128)(2,1)S(1)} collective-permute-done((bf16[8,128,128]{2,1,0:T(8,128)(2,1)S(1)}, bf16[8,128,128]{2,1,0:T(8,128)(2,1)S(1)}, u32[]{:S(2)}, u32[]{:S(2)}) %collective-permute-start.5) | collective-permute-done | bytes 262176 | tf_op jit(solution)/shard_map/ppermute | solution.py:22
  13.8 1.8 %collective-permute-start.6 = (bf16[8,128,128]{2,1,0:T(8,128)(2,1)S(1)}, bf16[8,128,128]{2,1,0:T(8,128)(2,1)S(1)}, u32[]{:S(2)}, u32[]{:S(2)}) collective-permute-start(bf16[8,128,128]{2,1,0:T(8,128)(2,1)S(1)} %collective-permute-done.5.refs_3_), channel_id=1, source_target_pairs={{0,8},{1,5},{2,10},{3,7},{8,16},{9,1},{10,18},{11,3},{16,24},{17,9... | collective-permute-start | bytes 786440 | tf_op jit(solution)/shard_map/ppermute | solution.py:22
  15.6 0.0 collective-permute-start.1
  15.6 1.5 %collective-permute-done.7.refs_2_ = bf16[8,128,128]{2,1,0:T(8,128)(2,1)S(1)} collective-permute-done((bf16[8,128,128]{2,1,0:T(8,128)(2,1)S(1)}, bf16[8,128,128]{2,1,0:T(8,128)(2,1)S(1)}, u32[]{:S(2)}, u32[]{:S(2)}) %collective-permute-start.7) | collective-permute-done | bytes 262176 | tf_op jit(solution)/shard_map/ppermute | solution.py:22
  17.1 2.1 %collective-permute-start.10 = (bf16[8,128,128]{2,1,0:T(8,128)(2,1)S(1)}, bf16[8,128,128]{2,1,0:T(8,128)(2,1)S(1)}, u32[]{:S(2)}, u32[]{:S(2)}) collective-permute-start(bf16[8,128,128]{2,1,0:T(8,128)(2,1)S(1)} %collective-permute-done.7.refs_2_), channel_id=1, source_target_pairs={{0,8},{1,5},{2,10},{3,7},{8,16},{9,1},{10,18},{11,3},{16,24},{17,9... | collective-permute-start | bytes 786440 | tf_op jit(solution)/shard_map/ppermute | solution.py:22
  19.1 1.0 %collective-permute-done.6.refs_1_ = bf16[8,128,128]{2,1,0:T(8,128)(2,1)S(1)} collective-permute-done((bf16[8,128,128]{2,1,0:T(8,128)(2,1)S(1)}, bf16[8,128,128]{2,1,0:T(8,128)(2,1)S(1)}, u32[]{:S(2)}, u32[]{:S(2)}) %collective-permute-start.6) | collective-permute-done | bytes 262176 | tf_op jit(solution)/shard_map/ppermute | solution.py:22
  20.1 1.8 %collective-permute-start.8 = (bf16[8,128,128]{2,1,0:T(8,128)(2,1)S(1)}, bf16[8,128,128]{2,1,0:T(8,128)(2,1)S(1)}, u32[]{:S(2)}, u32[]{:S(2)}) collective-permute-start(bf16[8,128,128]{2,1,0:T(8,128)(2,1)S(1)} %collective-permute-done.6.refs_1_), channel_id=1, source_target_pairs={{0,8},{1,5},{2,10},{3,7},{8,16},{9,1},{10,18},{11,3},{16,24},{17,9... | collective-permute-start | bytes 786440 | tf_op jit(solution)/shard_map/ppermute | solution.py:22
  21.9 0.0 collective-permute-done.1
  22.0 0.0 collective-permute-done.11.refs_6_.refs_3_
  22.0 2.4 %shard_map.55 = (f32[16,128,128]{2,1,0:T(8,128)S(1)}, f32[16,128,128]{2,1,0:T(8,128)S(1)}) custom-call(s32[5,16]{1,0:T(8,128)S(1)} %stack.13.refs_0_, bf16[8,128,128]{2,1,0:T(8,128)(2,1)S(1)} %bitcast.9, bf16[8,128,128]{2,1,0:T(8,128)(2,1)S(1)} %bitcast.7, bf16[8,128,128]{2,1,0:T(8,128)(2,1)S(1)} %collective-permute-done.5.refs_3_, ...), custom_call_target="tpu_custom_call" | custom-call | flops 805306368 | bytes 4194624 | tf_op jit(solution)/shard_map/pallas_call | solution.py:88
  24.4 0.0 collective-permute-done.10.refs_4_
  24.5 1.6 %collective-permute-start.12 = (bf16[4,128,128]{2,1,0:T(8,128)(2,1)S(1)}, bf16[4,128,128]{2,1,0:T(8,128)(2,1)S(1)}, u32[]{:S(2)}, u32[]{:S(2)}) collective-permute-start(bf16[4,128,128]{2,1,0:T(8,128)(2,1)S(1)} %constant_dynamic-slice_fusion), channel_id=1, source_target_pairs={{0,8},{1,5},{2,10},{3,7},{8,16},{9,1},{10,18},{11,3},{16,24},{17,9... | collective-permute-start | bytes 393224 | tf_op jit(solution)/shard_map/ppermute | solution.py:22
  26.1 0.4 %collective-permute-done.8.refs_3_ = bf16[8,128,128]{2,1,0:T(8,128)(2,1)S(1)} collective-permute-done((bf16[8,128,128]{2,1,0:T(8,128)(2,1)S(1)}, bf16[8,128,128]{2,1,0:T(8,128)(2,1)S(1)}, u32[]{:S(2)}, u32[]{:S(2)}) %collective-permute-start.8) | collective-permute-done | bytes 262176 | tf_op jit(solution)/shard_map/ppermute | solution.py:22
  26.5 1.9 %collective-permute-start.9 = (bf16[4,128,128]{2,1,0:T(8,128)(2,1)S(1)}, bf16[4,128,128]{2,1,0:T(8,128)(2,1)S(1)}, u32[]{:S(2)}, u32[]{:S(2)}) collective-permute-start(bf16[4,128,128]{2,1,0:T(8,128)(2,1)S(1)} %constant_dynamic-slice_fusion.1), channel_id=1, source_target_pairs={{0,8},{1,5},{2,10},{3,7},{8,16},{9,1},{10,18},{11,3},{16,24},{17,9... | collective-permute-start | bytes 393224 | tf_op jit(solution)/shard_map/ppermute | solution.py:22
  28.4 3.2 %shard_map.56 = (f32[16,128,128]{2,1,0:T(8,128)S(1)}, f32[16,128,128]{2,1,0:T(8,128)S(1)}) custom-call(s32[5,16]{1,0:T(8,128)S(1)} %stack.13.refs_0_, bf16[8,128,128]{2,1,0:T(8,128)(2,1)S(1)} %collective-permute-done.6.refs_1_, bf16[8,128,128]{2,1,0:T(8,128)(2,1)S(1)} %collective-permute-done.7.refs_2_, ...), custom_call_target="tpu_custom_call", output_to_operand_aliasing={{0}: (7, {}), {1}: (8, {})} | custom-call | flops 1073741824 | bytes 6291776 | tf_op jit(solution)/shard_map/pallas_call | solution.py:88
  31.6 0.0 collective-permute-done.12.refs_2_
  31.6 0.0 collective-permute-done.9.refs_1_
  31.6 1.0 %shard_map.58 = bf16[16,128,128]{2,1,0:T(8,128)(2,1)S(1)} custom-call(s32[5,16]{1,0:T(8,128)S(1)} %stack.13.refs_0_, bf16[4,128,128]{2,1,0:T(8,128)(2,1)S(1)} %collective-permute-done.9.refs_1_, bf16[4,128,128]{2,1,0:T(8,128)(2,1)S(1)} %collective-permute-done.12.refs_2_, bf16[16,128,128]{2,1,0:T(8,128)(2,1)S(1)} %collective-permute-done.11.refs_6_.refs_3_, ...), custom_call_target="tpu_custom_call" | custom-call | flops 134217728 | bytes 2883904 | tf_op jit(solution)/shard_map/pallas_call | solution.py:88
  32.7 0.1 collective-permute-start.13
  32.8 1.1 %shard_map.57 = f32[16,128,128]{2,1,0:T(8,128)S(1)} custom-call(s32[5,16]{1,0:T(8,128)S(1)} %stack.13.refs_0_, bf16[4,128,128]{2,1,0:T(8,128)(2,1)S(1)} %collective-permute-done.9.refs_1_, bf16[4,128,128]{2,1,0:T(8,128)(2,1)S(1)} %collective-permute-done.12.refs_2_, bf16[16,128,128]{2,1,0:T(8,128)(2,1)S(1)} %copy-done, ...), custom_call_target="tpu_custom_call", output_to_operand_aliasing={{}: (4, {})} | custom-call | flops 134217728 | bytes 2883904 | tf_op jit(solution)/shard_map/pallas_call | solution.py:88
  33.8 0.8 %collective-permute-done.13 = bf16[16,128,128]{2,1,0:T(8,128)(2,1)S(1)} collective-permute-done((bf16[16,128,128]{2,1,0:T(8,128)(2,1)S(1)}, bf16[16,128,128]{2,1,0:T(8,128)(2,1)S(1)}, u32[]{:S(2)}, u32[]{:S(2)}) %collective-permute-start.13) | collective-permute-done | bytes 524320 | tf_op jit(solution)/shard_map/ppermute | solution.py:27
  34.7 1.0 %add_convert_fusion = bf16[16,128,128]{2,1,0:T(8,128)(2,1)} fusion(f32[16,128,128]{2,1,0:T(8,128)S(1)} %shard_map.57, bf16[16,128,128]{2,1,0:T(8,128)(2,1)S(1)} %collective-permute-done.13), kind=kLoop, calls=%fused_computation | loop fusion | flops 786432 | bytes 2097152 | tf_op jit(solution)/shard_map/convert_element_type | solution.py:157
  (11 shorter events, 0.1 us)
Async XLA Ops:
  0.0 6.4 %collective-permute-start.3 = (bf16[2,1,128,128]{3,2,1,0:T(8,128)(2,1)}, bf16[2,1,128,128]{3,2,1,0:T(8,128)(2,1)S(1)}, u32[]{:S(2)}, u32[]{:S(2)}) collective-permute-start(bf16[2,1,128,128]{3,2,1,0:T(8,128)(2,1)} %param.8), channel_id=1, source_target_pairs={{0,2},{1,3},{2,0},{3,1},{4,6},{5,7},{6,4},{7,5},{8,10},{9,11},{10,... | collective-permute-start | bytes 196616 | tf_op jit(solution)/shard_map/ppermute | solution.py:27
  2.9 4.3 %collective-permute-start.4 = (bf16[2,1,128,128]{3,2,1,0:T(8,128)(2,1)}, bf16[2,1,128,128]{3,2,1,0:T(8,128)(2,1)S(1)}, u32[]{:S(2)}, u32[]{:S(2)}) collective-permute-start(bf16[2,1,128,128]{3,2,1,0:T(8,128)(2,1)} %param.8), channel_id=1, source_target_pairs={{0,3},{1,2},{2,1},{3,0},{4,7},{5,6},{6,5},{7,4},{8,11},{9,10},{10,... | collective-permute-start | bytes 196616 | tf_op jit(solution)/shard_map/ppermute | solution.py:27
  2.9 4.4 %collective-permute-start.2 = (bf16[2,1,128,128]{3,2,1,0:T(8,128)(2,1)}, bf16[2,1,128,128]{3,2,1,0:T(8,128)(2,1)S(1)}, u32[]{:S(2)}, u32[]{:S(2)}) collective-permute-start(bf16[2,1,128,128]{3,2,1,0:T(8,128)(2,1)} %param.8), channel_id=1, source_target_pairs={{0,1},{1,0},{2,3},{3,2},{4,5},{5,4},{6,7},{7,6},{8,9},{9,8},{10,11... | collective-permute-start | bytes 196616 | tf_op jit(solution)/shard_map/ppermute | solution.py:27
  3.1 3.3 %copy-start.1 = (bf16[2,1,128,128]{3,2,1,0:T(8,128)(2,1)S(1)}, bf16[2,1,128,128]{3,2,1,0:T(8,128)(2,1)}, u32[]{:S(2)}) copy-start(bf16[2,1,128,128]{3,2,1,0:T(8,128)(2,1)} %param.8) | copy-start | bytes 196612
  4.2 6.4 %collective-permute-start = (bf16[8,128,128]{2,1,0:T(8,128)(2,1)S(1)}, bf16[8,128,128]{2,1,0:T(8,128)(2,1)S(1)}, u32[]{:S(2)}, u32[]{:S(2)}) collective-permute-start(bf16[8,128,128]{2,1,0:T(8,128)(2,1)S(1)} %bitcast.6), channel_id=1, source_target_pairs={{0,8},{1,5},{2,10},{3,7},{8,16},{9,1},{10,18},{11,3},{16,24},{17,9... | collective-permute-start | bytes 786440 | tf_op jit(solution)/shard_map/ppermute | solution.py:22
  6.4 4.3 %copy-start = (bf16[16,128,128]{2,1,0:T(8,128)(2,1)S(1)}, bf16[16,128,128]{2,1,0:T(8,128)(2,1)}, u32[]{:S(2)}) copy-start(bf16[16,128,128]{2,1,0:T(8,128)(2,1)} %refs_3_.1) | copy-start | bytes 1572868
  7.3 6.4 %collective-permute-start.5 = (bf16[8,128,128]{2,1,0:T(8,128)(2,1)S(1)}, bf16[8,128,128]{2,1,0:T(8,128)(2,1)S(1)}, u32[]{:S(2)}, u32[]{:S(2)}) collective-permute-start(bf16[8,128,128]{2,1,0:T(8,128)(2,1)S(1)} %bitcast.8), channel_id=1, source_target_pairs={{0,8},{1,5},{2,10},{3,7},{8,16},{9,1},{10,18},{11,3},{16,24},{17,9... | collective-permute-start | bytes 786440 | tf_op jit(solution)/shard_map/ppermute | solution.py:22
  9.0 0.7 %copy-start.2 = (s32[16]{0:T(128)S(1)}, s32[16]{0:T(128)}, u32[]{:S(2)}) copy-start(s32[16]{0:T(128)} %param.7) | copy-start | bytes 196
  9.0 0.7 %copy-start.3 = (s32[16,1]{0,1:T(1,128)S(1)}, s32[16,1]{0,1:T(1,128)}, u32[]{:S(2)}) copy-start(s32[16,1]{0,1:T(1,128)} %param.6) | copy-start | bytes 196
  10.7 11.3 %collective-permute-start.11 = (bf16[16,128,128]{2,1,0:T(8,128)(2,1)S(1)}, bf16[16,128,128]{2,1,0:T(8,128)(2,1)S(1)}, u32[]{:S(2)}, u32[]{:S(2)}) collective-permute-start(bf16[16,128,128]{2,1,0:T(8,128)(2,1)S(1)} %copy-done), channel_id=1, source_target_pairs={{0,1},{1,0},{2,3},{3,2},{4,5},{5,4},{6,7},{7,6},{8,9},{9,8},{10,11... | collective-permute-start | bytes 1572872 | tf_op jit(solution)/shard_map/ppermute | solution.py:27
  10.7 6.4 %collective-permute-start.7 = (bf16[8,128,128]{2,1,0:T(8,128)(2,1)S(1)}, bf16[8,128,128]{2,1,0:T(8,128)(2,1)S(1)}, u32[]{:S(2)}, u32[]{:S(2)}) collective-permute-start(bf16[8,128,128]{2,1,0:T(8,128)(2,1)S(1)} %collective-permute-done.refs_4_), channel_id=1, source_target_pairs={{0,8},{1,5},{2,10},{3,7},{8,16},{9,1},{10,18},{11,3},{16,24},{17,9... | collective-permute-start | bytes 786440 | tf_op jit(solution)/shard_map/ppermute | solution.py:22
  13.8 6.4 %collective-permute-start.6 = (bf16[8,128,128]{2,1,0:T(8,128)(2,1)S(1)}, bf16[8,128,128]{2,1,0:T(8,128)(2,1)S(1)}, u32[]{:S(2)}, u32[]{:S(2)}) collective-permute-start(bf16[8,128,128]{2,1,0:T(8,128)(2,1)S(1)} %collective-permute-done.5.refs_3_), channel_id=1, source_target_pairs={{0,8},{1,5},{2,10},{3,7},{8,16},{9,1},{10,18},{11,3},{16,24},{17,9... | collective-permute-start | bytes 786440 | tf_op jit(solution)/shard_map/ppermute | solution.py:22
  15.6 6.4 %collective-permute-start.1 = (s32[2,16]{1,0:T(2,128)S(1)}, s32[2,16]{1,0:T(2,128)S(1)}, u32[]{:S(2)}, u32[]{:S(2)}) collective-permute-start(s32[2,16]{1,0:T(2,128)S(1)} %pad_add_fusion), channel_id=1, source_target_pairs={{0,1},{1,0},{2,3},{3,2},{4,5},{5,4},{6,7},{7,6},{8,9},{9,8},{10,11... | collective-permute-start | bytes 392 | tf_op jit(solution)/shard_map/ppermute | solution.py:27
  17.1 7.4 %collective-permute-start.10 = (bf16[8,128,128]{2,1,0:T(8,128)(2,1)S(1)}, bf16[8,128,128]{2,1,0:T(8,128)(2,1)S(1)}, u32[]{:S(2)}, u32[]{:S(2)}) collective-permute-start(bf16[8,128,128]{2,1,0:T(8,128)(2,1)S(1)} %collective-permute-done.7.refs_2_), channel_id=1, source_target_pairs={{0,8},{1,5},{2,10},{3,7},{8,16},{9,1},{10,18},{11,3},{16,24},{17,9... | collective-permute-start | bytes 786440 | tf_op jit(solution)/shard_map/ppermute | solution.py:22
  20.1 6.4 %collective-permute-start.8 = (bf16[8,128,128]{2,1,0:T(8,128)(2,1)S(1)}, bf16[8,128,128]{2,1,0:T(8,128)(2,1)S(1)}, u32[]{:S(2)}, u32[]{:S(2)}) collective-permute-start(bf16[8,128,128]{2,1,0:T(8,128)(2,1)S(1)} %collective-permute-done.6.refs_1_), channel_id=1, source_target_pairs={{0,8},{1,5},{2,10},{3,7},{8,16},{9,1},{10,18},{11,3},{16,24},{17,9... | collective-permute-start | bytes 786440 | tf_op jit(solution)/shard_map/ppermute | solution.py:22
  24.5 7.2 %collective-permute-start.12 = (bf16[4,128,128]{2,1,0:T(8,128)(2,1)S(1)}, bf16[4,128,128]{2,1,0:T(8,128)(2,1)S(1)}, u32[]{:S(2)}, u32[]{:S(2)}) collective-permute-start(bf16[4,128,128]{2,1,0:T(8,128)(2,1)S(1)} %constant_dynamic-slice_fusion), channel_id=1, source_target_pairs={{0,8},{1,5},{2,10},{3,7},{8,16},{9,1},{10,18},{11,3},{16,24},{17,9... | collective-permute-start | bytes 393224 | tf_op jit(solution)/shard_map/ppermute | solution.py:22
  26.5 5.1 %collective-permute-start.9 = (bf16[4,128,128]{2,1,0:T(8,128)(2,1)S(1)}, bf16[4,128,128]{2,1,0:T(8,128)(2,1)S(1)}, u32[]{:S(2)}, u32[]{:S(2)}) collective-permute-start(bf16[4,128,128]{2,1,0:T(8,128)(2,1)S(1)} %constant_dynamic-slice_fusion.1), channel_id=1, source_target_pairs={{0,8},{1,5},{2,10},{3,7},{8,16},{9,1},{10,18},{11,3},{16,24},{17,9... | collective-permute-start | bytes 393224 | tf_op jit(solution)/shard_map/ppermute | solution.py:22
  32.7 2.0 %collective-permute-start.13 = (bf16[16,128,128]{2,1,0:T(8,128)(2,1)S(1)}, bf16[16,128,128]{2,1,0:T(8,128)(2,1)S(1)}, u32[]{:S(2)}, u32[]{:S(2)}) collective-permute-start(bf16[16,128,128]{2,1,0:T(8,128)(2,1)S(1)} %shard_map.58), channel_id=1, source_target_pairs={{0,1},{1,0},{2,3},{3,2},{4,5},{5,4},{6,7},{7,6},{8,9},{9,8},{10,11... | collective-permute-start | bytes 1572872 | tf_op jit(solution)/shard_map/ppermute | solution.py:27
